TPU v7x, 32 devices: a whole 2x2x4 slice. The times are simulated.
32 devices in a mesh: segment: 4 (over z), dp: 2 (over x), tensor: 4 (over y, core).
Axes of the slice: x: 2, y: 2, z: 4, core: 2. Of those that a mesh axis runs over, the one named last changes fastest.
Arguments:
- inbound: bfloat16 [4, 2, 512, 4096], P('segment', None, 'dp'), may hold values from -21 to 21
- weights: bfloat16 [4, 4096, 3, 4096], P('segment', None, None, 'tensor'), may hold values from -0.09375 to 0.09375
- cotangent: bfloat16 [4, 2, 512, 4096], P('segment', None, 'dp', 'tensor'), may hold values from -20 to 20
Outputs:
- section_out: bfloat16 [4, 2, 512, 4096], P('segment', None, 'dp', 'tensor')
All inputs are finite; a program needn't handle non-finite values.
Results may differ from a plain program's by a relative error of at most 0.022.
The roundings to bfloat16 on the way count: a program that leaves them out, or rounds other values in their place, can miss the bound.
Values may be sent and summed in bfloat16 or wider, within the bound.
A program may use at most 128 MiB of HBM per device.

v0:
```python
import jax
import jax.numpy as jnp
from jax import lax
from jax.sharding import PartitionSpec as P

HD = 64


def broadcast(value, axis, root):
    mine = lax.axis_index(axis) == root
    return lax.psum(jnp.where(mine, value, jnp.zeros_like(value)), axis)


def shards(inbound, weights, cotangent):
    states = inbound[0]
    micro_count, row_count, model_width = states.shape
    encoded = broadcast(states, "segment", 0)
    section_layer = weights[0]
    feat_width = section_layer.shape[2]
    head_count = feat_width // HD
    score_scale = HD ** (-0.5)
    query = jnp.dot(
        states.reshape(micro_count * row_count, model_width),
        section_layer[:, 0, :],
        preferred_element_type=jnp.float32,
    ).astype(jnp.bfloat16)
    query = query.reshape(micro_count, row_count, feat_width)
    upstream = cotangent[0]
    pair_weights = section_layer[:, 1:, :].reshape(model_width, 2 * feat_width)
    keyval = jnp.dot(
        encoded.reshape(micro_count * row_count, model_width),
        pair_weights,
        preferred_element_type=jnp.float32,
    ).astype(jnp.bfloat16)
    keyval = keyval.reshape(micro_count, row_count, 2, feat_width)
    all_keyval = lax.all_gather(keyval, "dp", axis=1, tiled=True)
    key_count = all_keyval.shape[1]
    all_query, all_upstream = (query, upstream)
    query_count = all_query.shape[1]

    def attend(items):
        query_one, upstream_one, keyval_one = items
        query_heads = query_one.reshape(query_count, head_count, HD)
        grad_heads = upstream_one.reshape(query_count, head_count, HD)
        key_heads = keyval_one[:, 0].reshape(key_count, head_count, HD)
        value_heads = keyval_one[:, 1].reshape(key_count, head_count, HD)
        scores = (
            jnp.einsum("qhe,khe->hqk", query_heads, key_heads, preferred_element_type=jnp.float32)
            * score_scale
        )
        score_peak = jnp.max(scores, axis=-1, keepdims=True)
        exp_scores = jnp.exp(scores - score_peak)
        attend_prob = exp_scores / jnp.sum(exp_scores, axis=-1, keepdims=True)
        prob_rounded = attend_prob.astype(jnp.bfloat16)
        prob_grad = jnp.einsum(
            "qhe,khe->hqk", grad_heads, value_heads, preferred_element_type=jnp.float32
        )
        row_delta = jnp.sum(attend_prob * prob_grad, axis=-1, keepdims=True)
        score_grad = (attend_prob * (prob_grad - row_delta) * score_scale).astype(jnp.bfloat16)
        context = jnp.einsum(
            "hqk,khe->qhe", prob_rounded, value_heads, preferred_element_type=jnp.float32
        )
        key_grad = jnp.einsum(
            "hqk,qhe->khe", score_grad, query_heads, preferred_element_type=jnp.float32
        )
        value_grad = jnp.einsum(
            "hqk,qhe->khe", prob_rounded, grad_heads, preferred_element_type=jnp.float32
        )
        context = context.astype(jnp.bfloat16).reshape(row_count, feat_width)
        joined = jnp.stack(
            [key_grad.reshape(-1, feat_width), value_grad.reshape(-1, feat_width)], axis=1
        )
        return (context, joined)

    context, joined_grads = lax.map(attend, (all_query, all_upstream, all_keyval))
    owned_grads = lax.psum_scatter(joined_grads, "dp", scatter_dimension=1, tiled=True).astype(
        jnp.bfloat16
    )
    head_terms = jnp.einsum(
        "rc,dc->rd",
        owned_grads.reshape(micro_count * row_count, 2 * feat_width),
        pair_weights,
        preferred_element_type=jnp.float32,
    )
    head_terms = head_terms.reshape(micro_count, row_count, model_width)
    heads_total = lax.psum_scatter(
        head_terms.astype(jnp.bfloat16), "tensor", scatter_dimension=2, tiled=True
    ).astype(jnp.float32)
    segment_index = lax.axis_index("segment")
    live_mask = (segment_index > 0).astype(jnp.float32)
    sections = lax.psum(heads_total * live_mask, "segment")
    encoder_grad = (sections + cotangent[0].astype(jnp.float32)).astype(jnp.bfloat16)
    result = jnp.where(segment_index == 0, encoder_grad, context)
    return result[None]


def solution(mesh):
    placed = (
        P("segment", None, "dp", None),
        P("segment", None, None, "tensor"),
        P("segment", None, "dp", "tensor"),
    )
    return jax.shard_map(
        shards,
        mesh=mesh,
        in_specs=placed,
        out_specs=P("segment", None, "dp", "tensor"),
        check_vma=False,
    )
```

profile of v0, /device:TPU:0, one launch (start us, length us, event | category | flops | bytes accessed | tf_op | source)
XLA Modules:
  0.0 623.3 jit_solution(14302715760011410353)
XLA Ops:
  6.5 0.0 all-reduce.3.cloned.1.call-start
  6.5 4.4 broadcast_select_fusion
  10.9 0.0 all-reduce.3.cloned.1.call-update
  11.0 0.0 all-gather.2.cloned.1.call-start
  11.0 14.0 %slice.16 = bf16[4096,2,1024]{2,0,1:T(8,128)(2,1)} slice(bf16[4096,3,1024]{2,0,1:T(8,128)(2,1)} %bitcast.99), slice={[0:4096], [1:3], [0:1024]} | slice | bytes 33554432 | tf_op jit(solution)/shard_map/slice | solution.py:29
  25.0 20.7 %copy.9 = bf16[4096,2,1024]{0,2,1:T(8,128)(2,1)} copy(bf16[4096,2,1024]{2,0,1:T(8,128)(2,1)} %slice.16) | data formatting | bytes 33554432 | tf_op jit(solution)/shard_map/slice | solution.py:29
  45.7 121.7 %all-reduce.3.cloned.1.call-done = bf16[512,4096]{1,0:T(8,128)(2,1)} async-done(((bf16[512,4096]{1,0:T(8,128)(2,1)}), bf16[512,4096]{1,0:T(8,128)(2,1)}) %all-reduce.3.cloned.1.call-update) | async-done | bytes 4194320 | tf_op jit(solution)/shard_map/psum | solution.py:11
  167.4 14.7 %convolution_convert_fusion = bf16[512,2048]{1,0:T(8,128)(2,1)} fusion(bf16[512,4096]{1,0:T(8,128)(2,1)} %all-reduce.3.cloned.1.call-done, bf16[4096,2048]{0,1:T(8,128)(2,1)} %bitcast.92), kind=kOutput, calls=%fused_computation.33 | convolution fusion | flops 8590983168 | bytes 23068672 | tf_op jit(solution)/shard_map/dot_general | solution.py:30
  182.1 3.3 reshape.40
  185.4 4.1 copy.10
  189.5 0.0 all-gather.2.cloned.1.call-update
  189.5 0.2 reduce-scatter.3.cloned.1.call-start
  189.8 10.1 %fusion.32 = bf16[512,1024]{1,0:T(8,128)(2,1)} fusion(bf16[512,4096]{1,0:T(8,128)(2,1)} %bitcast.103, bf16[4096,3,1024]{2,0,1:T(8,128)(2,1)} %bitcast.100), kind=kOutput, calls=%fused_computation.37 | convolution fusion | flops 4295491584 | bytes 13631488 | tf_op jit(solution)/shard_map/dot_general | solution.py:22
  199.9 45.5 %all-gather.2.cloned.1.call-done = bf16[2,512,2,1024]{1,3,2,0:T(8,128)(2,1)} async-done(((bf16[2,256,2,1024]{1,3,2,0:T(8,128)(2,1)}), bf16[2,512,2,1024]{1,3,2,0:T(8,128)(2,1)}) %all-gather.2.cloned.1.call-update) | async-done | bytes 4194320 | tf_op jit(solution)/shard_map/all_gather | solution.py:36
  245.4 119.5 %while.12 = (s32[]{:T(128)}, bf16[2,256,1024]{2,1,0:T(8,128)(2,1)}, f32[2,512,2,1024]{1,3,2,0:T(8,128)}, bf16[2,512,2,1024]{1,3,2,0:T(8,128)(2,1)}, bf16[2,256,1...) while((s32[]{:T(128)}, bf16[2,256,1024]{2,1,0:T(8,128)(2,1)}, ...), condition=%wide.region_5.6_spmd, body=%wide.region_1.5_spmd.sunk | while | flops 1372853248 | bytes 96011400 | solution.py:75
  245.4 0.0 copy-start.2
  245.4 1.8 dynamic-slice_bitcast_fusion.2
  247.2 0.1 fusion.78
  247.4 0.0 copy-done.2
  247.4 0.2 copy.24
  247.6 4.8 fusion.79
  252.5 4.9 fusion.80
  257.3 0.2 copy.25
  257.5 1.9 constant_dynamic-slice_fusion.5
  259.4 0.2 copy.26
  259.7 4.5 fusion.82
  264.2 34.4 %fusion.83 = f32[16,64,512]{2,1,0:T(8,128)} fusion(bf16[256,16,64]{0,2,1:T(8,128)(2,1)S(1)} %bitcast.95, f32[16,256,512]{2,1,0:T(8,128)} %fusion.82, f32[16,256,512]{2,1,0:T(8,128)} %get-tuple-element.115, f32[16,256]{1,0:T(8,128)S(1)} %get-tuple-element.116), kind=kOutput, calls=%fused_computation.8.clone.1 | convolution fusion | flops 283120128 | bytes 19415040 | tf_op jit(solution)/shard_map/while/body/eval_jaxpr/hqk,qhe->khe/dot_general | solution.py:63
  298.6 0.0 copy-start
  298.6 4.2 fusion.81
  302.8 0.0 copy-done
  302.8 2.4 fusion.84
  305.2 0.0 copy-start.2
  305.2 1.8 dynamic-slice_bitcast_fusion.2
  307.0 0.1 fusion.78
  307.1 0.0 copy-done.2
  307.2 0.2 copy.24
  307.4 4.8 fusion.79
  312.2 4.9 fusion.80
  317.1 0.2 copy.25
  317.3 1.9 constant_dynamic-slice_fusion.5
  319.2 0.2 copy.26
  319.4 4.5 fusion.82
  323.9 34.4 %fusion.83 = f32[16,64,512]{2,1,0:T(8,128)} fusion(bf16[256,16,64]{0,2,1:T(8,128)(2,1)S(1)} %bitcast.95, f32[16,256,512]{2,1,0:T(8,128)} %fusion.82, f32[16,256,512]{2,1,0:T(8,128)} %get-tuple-element.115, f32[16,256]{1,0:T(8,128)S(1)} %get-tuple-element.116), kind=kOutput, calls=%fused_computation.8.clone.1 | convolution fusion | flops 283120128 | bytes 19415040 | tf_op jit(solution)/shard_map/while/body/eval_jaxpr/hqk,qhe->khe/dot_general | solution.py:63
  358.3 0.0 copy-start
  358.3 4.2 fusion.81
  362.5 0.0 copy-done
  362.5 2.4 fusion.84
  364.9 0.0 reduce-scatter.3.cloned.1.call-update
  365.0 0.3 reduce-scatter.5.cloned.1.call-start
  365.2 99.1 %reduce-scatter.3.cloned.1.call-done = f32[2,256,2,1024]{1,3,2,0:T(8,128)} async-done(((f32[2,512,2,1024]{1,3,2,0:T(8,128)}), f32[2,256,2,1024]{1,3,2,0:T(8,128)}) %reduce-scatter.3.cloned.1.call-update) | async-done | bytes 4194320 | tf_op jit(solution)/shard_map/reduce_scatter | solution.py:76
  464.3 15.1 %bitcast_convert_fusion = bf16[2,256,4096]{2,1,0:T(8,128)(2,1)} fusion(f32[2,256,2,1024]{1,3,2,0:T(8,128)} %reduce-scatter.3.cloned.1.call-done, bf16[4096,3,1024]{2,0,1:T(8,128)(2,1)} %bitcast.101), kind=kOutput, calls=%fused_computation.31 | convolution fusion | flops 8593080320 | bytes 25165824 | tf_op jit(solution)/shard_map/rc,dc->rd/dot_general | solution.py:79
  479.5 0.0 copy-start.1
  479.5 0.0 copy-start.3
  479.5 0.0 reduce-scatter.5.cloned.1.call-update
  479.5 0.0 all-reduce.5.cloned.1.call-start
  479.6 44.6 %reduce-scatter.5.cloned.1.call-done = bf16[2,256,1024]{2,1,0:T(8,128)(2,1)} async-done(((bf16[2,256,4096]{2,1,0:T(8,128)(2,1)}), bf16[2,256,1024]{2,1,0:T(8,128)(2,1)}) %reduce-scatter.5.cloned.1.call-update) | async-done | bytes 1048592 | tf_op jit(solution)/shard_map/reduce_scatter | solution.py:86
  524.2 2.8 convert_multiply_fusion
  527.0 0.0 all-reduce.5.cloned.1.call-update
  527.0 86.7 %all-reduce.5.cloned.1.call-done = f32[2,256,1024]{2,1,0:T(8,128)} async-done(((f32[2,256,1024]{2,1,0:T(8,128)}), f32[2,256,1024]{2,1,0:T(8,128)}) %all-reduce.5.cloned.1.call-update) | async-done | bytes 2097168 | tf_op jit(solution)/shard_map/psum | solution.py:91
  613.7 0.0 copy-done.1
  613.7 0.0 copy-done.3
  613.7 3.1 fusion.34
  (4 shorter events, 0.1 us)
Async XLA Ops:
  6.5 160.9 %all-reduce.3.cloned.1.call-start = ((), (), s32[]{:S(2)}) async-start(), calls=%async_computation.2 | async-start | bytes 8388608 | tf_op jit(solution)/shard_map/psum | solution.py:11
  11.0 234.4 %all-gather.2.cloned.1.call-start = ((), (), s32[]{:S(2)}) async-start(), calls=%async_computation.3 | async-start | bytes 6291456 | tf_op jit(solution)/shard_map/all_gather | solution.py:36
  189.5 274.8 %reduce-scatter.3.cloned.1.call-start = ((), (), s32[]{:S(2)}) async-start(), calls=%async_computation.4 | async-start | bytes 12582912 | tf_op jit(solution)/shard_map/reduce_scatter | solution.py:76
  245.4 2.0 copy-start.2
  298.6 4.2 copy-start
  305.2 2.0 copy-start.2
  358.3 4.2 copy-start
  365.0 159.2 %reduce-scatter.5.cloned.1.call-start = ((), (), s32[]{:S(2)}) async-start(), calls=%async_computation.5 | async-start | bytes 5242880 | tf_op jit(solution)/shard_map/reduce_scatter | solution.py:86
  479.5 134.2 %copy-start.1 = (bf16[2,256,1024]{2,1,0:T(8,128)(2,1)S(1)}, bf16[2,256,1024]{2,1,0:T(8,128)(2,1)}, u32[]{:S(2)}) copy-start(bf16[2,256,1024]{2,1,0:T(8,128)(2,1)} %get-tuple-element.148) | copy-start | bytes 3145732
  479.5 134.2 %copy-start.3 = (bf16[2,256,1024]{2,1,0:T(8,128)(2,1)S(1)}, bf16[2,256,1024]{2,1,0:T(8,128)(2,1)}, u32[]{:S(2)}) copy-start(bf16[2,256,1024]{2,1,0:T(8,128)(2,1)} %get-tuple-element.39) | copy-start | bytes 3145732
  479.5 134.2 %all-reduce.5.cloned.1.call-start = ((), (), s32[]{:S(2)}) async-start(), calls=%async_computation.6 | async-start | bytes 4194304 | tf_op jit(solution)/shard_map/psum | solution.py:91
Sparse Core Ops, SparseCore 0:
  11.1 156.2 all-reduce.2
  189.6 55.7 all-gather.1
  365.1 99.2 reduce-scatter.2
  479.6 44.4 reduce-scatter.4
  527.1 86.5 all-reduce.4
where the time goes:
time: 624 us; the launch traced here: 623 us
  waiting for transfers between devices  398 us (64%)
  matrix products  145 us (23%)
  local copies, waits for them, and re-layouts  51.2 us (8%)
  other arithmetic  15.1 us (2%)
  between operations  13.2 us (2%)
    psum x1, waiting for transfers between devices, broadcast(): return lax.psum(jnp.where(mine, value, jnp.zeros_like(value)), axis)  122 us
    reduce_scatter x1, waiting for transfers between devices, shards(): lax.psum_scatter(joined_grads, 'dp', scatter_dimension=1, tiled=True)  99.1 us
    psum x1, waiting for transfers between devices, shards(): sections = lax.psum(heads_total * live_mask, 'segment')  86.7 us
    dot_general x2, matrix products, attend(): jnp.einsum('hqk,qhe->khe', score_grad, query_heads, preferred_element_typ...  68.8 us
    all_gather x1, waiting for transfers between devices, shards(): all_keyval = lax.all_gather(keyval, 'dp', axis=1, tiled=True)  45.5 us
    reduce_scatter x1, waiting for transfers between devices, shards(): lax.psum_scatter(head_terms.astype(jnp.bfloat16), 'tensor', scatter_dimen...  44.6 us
    slice x2, local copies, waits for them, and re-layouts, shards(): pair_weights = section_layer[:, 1:, :].reshape(model_width, 2 * feat_width)  34.7 us
    dot_general x1, matrix products, shards(): jnp.einsum('rc,dc->rd', owned_grads.reshape(micro_count * row_count, 2 *...  15.1 us
  transfers between devices with their start and end apart: 5, of which 5 were waited for; matrix products, arithmetic and copies ran while one was open for 7% of the time, Pallas kernels for 0%

commit v1 on v0

--- a/solution.py
+++ b/solution.py
@@ -1,6 +1,8 @@
 import jax
 import jax.numpy as jnp
 from jax import lax
+from jax.experimental import pallas as pl
+from jax.experimental.pallas import tpu as pltpu
 from jax.sharding import PartitionSpec as P
 
 HD = 64
@@ -94,14 +96,458 @@
     return result[None]
 
 
+CHUNKS = 4
+
+
+def relay_kernel(n_segment, x_ref, w_ref, g_ref, out_ref,
+                 enc, own_x, wq, wkv, cot0, parts, ctx, rctx, dkv, rdkv,
+                 core_out, core_in, y_out, y_in, total, z_out, z_in,
+                 load_x, load_w, load_q, load_g,
+                 zs, zr, cs, cr, ys, yr, fs, fr, xs, xr, ds_, dr, ts, tr,
+                 ks, kr, vs, vr, us, ur):
+    micro, rows, width = x_ref.shape
+    feat = w_ref.shape[2]
+    half = feat // 2
+    quarter = half // 2
+    piece = rows // 4
+    crow = piece // CHUNKS
+    steps = micro * CHUNKS
+    zrow = rows // CHUNKS
+    pairs = half // 128
+
+    seg = lax.axis_index("segment")
+    d = lax.axis_index("dp")
+    t = lax.axis_index("tensor")
+    y, c = t // 2, t % 2
+    peer_x = {"dp": 1 - d}
+    peer_c = {"tensor": y * 2 + (1 - c)}
+    peer_y = {"tensor": (1 - y) * 2 + c}
+    up = {"segment": lax.min(seg + 1, n_segment - 1)}
+    down = {"segment": lax.max(seg - 1, 0)}
+    first, last = seg == 0, seg == n_segment - 1
+    MESH = pl.DeviceIdType.MESH
+
+    def remote(src, dst, s, r, dev):
+        return pltpu.make_async_remote_copy(
+            src_ref=src, dst_ref=dst, send_sem=s, recv_sem=r,
+            device_id=dev, device_id_type=MESH)
+
+    def slot(ref, who, j):
+        row = pl.multiple_of(who * piece + lax.rem(j, CHUNKS) * crow, crow)
+        return ref.at[j // CHUNKS, pl.ds(row, crow), :]
+
+    def z_copy(ref, j):
+        return remote(slot(ref, t, j), slot(enc, t, j), zs.at[j], zr.at[j], up)
+
+    def c_copy(j):
+        return remote(slot(enc, t, j), slot(enc, t, j), cs.at[j], cr.at[j], peer_c)
+
+    def y_copy(j):
+        return remote(slot(enc, t, j), slot(enc, t, j), ys.at[j], yr.at[j], peer_y)
+
+    ty = (1 - y) * 2 + c
+
+    def f_copy(j):
+        return remote(slot(enc, ty, j), slot(enc, ty, j), fs.at[j], fr.at[j], peer_c)
+
+    def lanes(which, size):
+        return pl.ds(pl.multiple_of(which * size, size), size)
+
+    def x_copy(kind, m):
+        i = kind * micro + m
+        return remote(parts.at[kind, m, 2], parts.at[kind, m, d], xs.at[i], xr.at[i], peer_x)
+
+    def g_copy(m):
+        i = 3 * micro + m
+        return remote(g_ref.at[m, :, lanes(1 - d, half)], parts.at[3, m, d],
+                      xs.at[i], xr.at[i], peer_x)
+
+    def g_load(m):
+        return pltpu.make_async_copy(g_ref.at[m, :, lanes(d, half)], parts.at[3, m, d], load_g.at[m])
+
+    def q_load(n):
+        h = jnp.where(n < 2, 1 - d, d)
+        col = pl.multiple_of(h * half + lax.rem(n, 2) * quarter, quarter)
+        b = lax.rem(n, 2)
+        return pltpu.make_async_copy(w_ref.at[0, :, pl.ds(col, quarter)], wq.at[b], load_q.at[b])
+
+    def w_load(k):
+        return pltpu.make_async_copy(w_ref.at[k + 1], wkv.at[k], load_w.at[k])
+
+    def d_copy(m, p):
+        i = m * pairs + p
+        lane = lanes(p, 128)
+        return remote(dkv.at[m, 1 - d, :, :, lane], rdkv.at[m, :, :, lane], ds_.at[i], dr.at[i], peer_x)
+
+    def t_copy(m, p):
+        i = m * pairs + p
+        lane = lanes(p, 128)
+        return remote(ctx.at[m, 1 - d, :, lane], rctx.at[m, :, lane], ts.at[i], tr.at[i], peer_x)
+
+    def k_copy(m, yy):
+        i = m * 2 + yy
+        return remote(core_out.at[m, yy], core_in.at[m, yy], ks.at[i], kr.at[i], peer_c)
+
+    def v_copy(i):
+        m, row = i // CHUNKS, pl.multiple_of(lax.rem(i, CHUNKS) * zrow, zrow)
+        return remote(y_out.at[m, pl.ds(row, zrow), :], y_in.at[m, pl.ds(row, zrow), :],
+                      vs.at[i], vr.at[i], peer_y)
+
+    def u_copy(i):
+        m, row = i // CHUNKS, pl.multiple_of(lax.rem(i, CHUNKS) * zrow, zrow)
+        return remote(z_out.at[m, pl.ds(row, zrow), :], z_in.at[m, pl.ds(row, zrow), :],
+                      us.at[i], ur.at[i], down)
+
+    x_load = pltpu.make_async_copy(x_ref, own_x, load_x)
+    c_load = pltpu.make_async_copy(g_ref, cot0, load_x)
+
+    barrier = pltpu.get_barrier_semaphore()
+    for dev in (peer_x, peer_c, peer_y):
+        pl.semaphore_signal(barrier, inc=1, device_id=dev, device_id_type=MESH)
+
+    @pl.when(jnp.logical_not(last))
+    def _():
+        pl.semaphore_signal(barrier, inc=1, device_id=up, device_id_type=MESH)
+
+    @pl.when(jnp.logical_not(first))
+    def _():
+        pl.semaphore_signal(barrier, inc=1, device_id=down, device_id_type=MESH)
+
+    ends = first.astype(jnp.int32) + last.astype(jnp.int32)
+    pl.semaphore_wait(barrier, 5 - ends)
+
+    @pl.when(first)
+    def _():
+        def send(j, carry):
+            z_copy(x_ref, j).start()
+            return carry
+        lax.fori_loop(0, steps, send, 0)
+        c_load.start()
+        c_load.wait()
+
+        def finish(i, carry):
+            u_copy(i).wait_recv()
+            m, row = i // CHUNKS, pl.multiple_of(lax.rem(i, CHUNKS) * zrow, zrow)
+            rr = pl.ds(row, zrow)
+            out_ref[m, rr, :] = (z_in[m, rr, :].astype(jnp.float32)
+                                 + cot0[m, rr, :].astype(jnp.float32)).astype(out_ref.dtype)
+            return carry
+        lax.fori_loop(0, steps, finish, 0)
+
+        def drain(j, carry):
+            z_copy(x_ref, j).wait_send()
+            return carry
+        lax.fori_loop(0, steps, drain, 0)
+
+    @pl.when(jnp.logical_not(first))
+    def _():
+        x_load.start()
+        q_load(0).start()
+        q_load(1).start()
+        for k in range(2):
+            w_load(k).start()
+        for m in range(micro):
+            g_load(m).start()
+            g_copy(m).start()
+
+        def forward(j):
+            z_copy(enc, j).wait_recv()
+
+            @pl.when(jnp.logical_not(last))
+            def _():
+                z_copy(enc, j).start()
+            y_copy(j).start()
+            c_copy(j).start()
+
+        def relay(j):
+            y_copy(j).wait_recv()
+            f_copy(j).start()
+
+        x_load.wait()
+
+        def q_step(j, carry):
+            q_load(j).wait()
+            value = jnp.dot(own_x[...].reshape(micro * rows, width), wq[lax.rem(j, 2)],
+                            preferred_element_type=jnp.float32)
+            value = (value * HD ** -0.5).astype(jnp.bfloat16).reshape(micro, rows, quarter)
+            where = jnp.where(j < 2, 2, d)
+            for m in range(micro):
+                parts[0, m, where, :, lanes(lax.rem(j, 2), quarter)] = value[m]
+
+            @pl.when(j < 2)
+            def _():
+                q_load(j + 2).start()
+
+            @pl.when(j == 1)
+            def _():
+                for m in range(micro):
+                    x_copy(0, m).start()
+            forward(j)
+
+            @pl.when(j > 0)
+            def _():
+                relay(j - 1)
+            return carry
+        lax.fori_loop(0, CHUNKS, q_step, 0)
+        for k in range(2):
+            w_load(k).wait()
+
+        def gathered(m):
+            def one(j, carry):
+                c_copy(j).wait_recv()
+                f_copy(j).wait_recv()
+                return carry
+            lax.fori_loop(m * CHUNKS, (m + 1) * CHUNKS, one, 0)
+
+        def kv_step(i, carry):
+            m, o = i // 4, lax.rem(i, 4)
+
+            @pl.when(m == 0)
+            def _():
+                forward(CHUNKS + i)
+                relay(CHUNKS + i - 1)
+
+            @pl.when(i == 0)
+            def _():
+                gathered(0)
+
+            @pl.when(i == 4)
+            def _():
+                relay(steps - 1)
+                gathered(1)
+            k = lax.rem(o, 2)
+            h = jnp.where(o < 2, 1 - d, d)
+            value = jnp.dot(enc[m], wkv[k, :, lanes(h, half)], preferred_element_type=jnp.float32)
+            parts[1 + k, m, jnp.where(o < 2, 2, d)] = value.astype(jnp.bfloat16)
+
+            @pl.when(o < 2)
+            def _():
+                x_copy(1 + k, m).start()
+            return carry
+        lax.fori_loop(0, 4 * micro, kv_step, 0)
+
+        lane_id = lax.broadcasted_iota(jnp.int32, (1, 128), 1)
+        f32 = jnp.float32
+
+        def attend(m, lo, hi):
+            def pair(p, carry):
+                lane = lanes(p, 128)
+                key = parts[1, m, 0:2, :, lane].reshape(2 * rows, 128)
+                val = parts[2, m, 0:2, :, lane].reshape(2 * rows, 128)
+                dk = jnp.zeros((2 * rows, 128), f32)
+                dv = jnp.zeros((2 * rows, 128), f32)
+                masks = [(lane_id < HD), (lane_id >= HD)]
+                zero = jnp.zeros((), jnp.bfloat16)
+                for b in range(2):
+                    qry = parts[0, m, b, :, lane]
+                    ups = parts[3, m, b, :, lane]
+                    acc = jnp.zeros((128, rows), f32)
+                    for mask in masks:
+                        km = jnp.where(mask, key, zero)
+                        vm = jnp.where(mask, val, zero)
+                        nt = (((1,), (1,)), ((), ()))
+                        sc = lax.dot_general(km, qry, nt, preferred_element_type=f32)
+                        dp = lax.dot_general(vm, ups, nt, preferred_element_type=f32)
+                        ex = jnp.exp(sc - jnp.max(sc, axis=0, keepdims=True))
+                        pr = ex * (1.0 / jnp.sum(ex, axis=0, keepdims=True))
+                        pb = pr.astype(jnp.bfloat16)
+                        delta = jnp.sum(pr * dp, axis=0, keepdims=True)
+                        sg = (pr * (dp - delta)).astype(jnp.bfloat16)
+                        acc = acc + lax.dot_general(vm, pb, (((0,), (0,)), ((), ())),
+                                                    preferred_element_type=f32)
+                        dv = dv + jnp.dot(pb, jnp.where(mask, ups, zero), preferred_element_type=f32)
+                        dk = dk + jnp.dot(sg, jnp.where(mask, qry, zero), preferred_element_type=f32)
+                    ctx[m, b, :, lane] = acc.T.astype(jnp.bfloat16)
+                dkb = dk.astype(jnp.bfloat16).reshape(2, rows, 128)
+                dvb = dv.astype(jnp.bfloat16).reshape(2, rows, 128)
+                for b in range(2):
+                    dkv[m, b, 0, :, lane] = dkb[b]
+                    dkv[m, b, 1, :, lane] = dvb[b]
+                d_copy(m, p).start()
+                t_copy(m, p).start()
+                return carry
+            lax.fori_loop(lo, hi, pair, 0)
+
+        def term(m, col):
+            value = None
+            for h, ref in ((d, dkv.at[m, d]), (1 - d, rdkv.at[m])):
+                for k in range(2):
+                    part = lax.dot_general(
+                        ref[k], wkv[k, pl.ds(pl.multiple_of(col, half), half), lanes(h, half)],
+                        (((1,), (1,)), ((), ())), preferred_element_type=f32)
+                    value = part if value is None else value + part
+            return value
+
+        def grads_out(m):
+            def got(p, carry):
+                d_copy(m, p).wait_recv()
+                return carry
+            lax.fori_loop(0, pairs, got, 0)
+
+            def tile(k, carry):
+                yy, o = k // 2, lax.rem(k, 2)
+                col = (yy * 2 + 1 - c) * feat + o * half
+                core_out[m, yy, :, lanes(o, half)] = term(m, col).astype(jnp.bfloat16)
+
+                @pl.when(o == 1)
+                def _():
+                    k_copy(m, yy).start()
+                return carry
+            lax.fori_loop(0, 4, tile, 0)
+
+        def grads_in(m):
+            def tile(k, carry):
+                o = lax.rem(k, 2)
+                yy = jnp.where(k < 2, 1 - y, y)
+
+                @pl.when(o == 0)
+                def _():
+                    k_copy(m, yy).wait_recv()
+                col = (yy * 2 + c) * feat + o * half
+                value = term(m, col) + core_in[m, yy, :, lanes(o, half)].astype(f32)
+
+                @pl.when(k < 2)
+                def _():
+                    y_out[m, :, lanes(o, half)] = value.astype(jnp.bfloat16)
+
+                @pl.when(k >= 2)
+                def _():
+                    total[m, :, lanes(o, half)] = value
+
+                @pl.when(k == 1)
+                def _():
+                    for q in range(CHUNKS):
+                        v_copy(m * CHUNKS + q).start()
+                return carry
+            lax.fori_loop(0, 4, tile, 0)
+
+        def got_parts(m):
+            for kind in range(3):
+                x_copy(kind, m).wait_recv()
+            g_copy(m).wait_recv()
+            g_load(m).wait()
+
+        got_parts(0)
+        attend(0, 0, pairs)
+        got_parts(1)
+        attend(1, 0, pairs // 2)
+        grads_out(0)
+        attend(1, pairs // 2, pairs)
+        grads_in(0)
+        grads_out(1)
+        grads_in(1)
+
+        def chain(i, carry):
+            m, row = i // CHUNKS, pl.multiple_of(lax.rem(i, CHUNKS) * zrow, zrow)
+            rr = pl.ds(row, zrow)
+            v_copy(i).wait_recv()
+            total[m, rr, :] = total[m, rr, :] + y_in[m, rr, :].astype(f32)
+
+            @pl.when(jnp.logical_not(last))
+            def _():
+                u_copy(i).wait_recv()
+                total[m, rr, :] = total[m, rr, :] + z_in[m, rr, :].astype(f32)
+            z_out[m, rr, :] = total[m, rr, :].astype(jnp.bfloat16)
+            u_copy(i).start()
+            return carry
+        lax.fori_loop(0, steps, chain, 0)
+
+        def context(i, carry):
+            t_copy(i // pairs, lax.rem(i, pairs)).wait_recv()
+            return carry
+        lax.fori_loop(0, micro * pairs, context, 0)
+        for m in range(micro):
+            out_ref[m, :, lanes(d, half)] = ctx[m, d]
+            out_ref[m, :, lanes(1 - d, half)] = rctx[m]
+
+        def drain(i, carry):
+            @pl.when(jnp.logical_not(last))
+            def _():
+                z_copy(enc, i).wait_send()
+            c_copy(i).wait_send()
+            y_copy(i).wait_send()
+            f_copy(i).wait_send()
+            v_copy(i).wait_send()
+            u_copy(i).wait_send()
+            return carry
+        lax.fori_loop(0, steps, drain, 0)
+
+        def drain_pairs(i, carry):
+            d_copy(i // pairs, lax.rem(i, pairs)).wait_send()
+            t_copy(i // pairs, lax.rem(i, pairs)).wait_send()
+            return carry
+        lax.fori_loop(0, micro * pairs, drain_pairs, 0)
+        for m in range(micro):
+            for kind in range(3):
+                x_copy(kind, m).wait_send()
+            g_copy(m).wait_send()
+            for yy in range(2):
+                k_copy(m, yy).wait_send()
+
+
+def fused_shards(n_segment, inbound, weights, cotangent):
+    micro, rows, width = inbound.shape[1:]
+    feat = weights.shape[3]
+    half = feat // 2
+    steps, pairs = micro * CHUNKS, half // 128
+    bf, f32 = jnp.bfloat16, jnp.float32
+    vm, dma = pltpu.VMEM, pltpu.SemaphoreType.DMA
+    scratch = [
+        vm((micro, rows, width), bf),
+        vm((micro, rows, width), bf),
+        vm((2, width, half // 2), bf),
+        vm((2, width, feat), bf),
+        vm((micro, rows, feat), bf),
+        vm((4, micro, 3, rows, half), bf),
+        vm((micro, 2, rows, half), bf),
+        vm((micro, rows, half), bf),
+        vm((micro, 2, 2, rows, half), bf),
+        vm((micro, 2, rows, half), bf),
+        vm((micro, 2, rows, feat), bf),
+        vm((micro, 2, rows, feat), bf),
+        vm((micro, rows, feat), bf),
+        vm((micro, rows, feat), bf),
+        vm((micro, rows, feat), f32),
+        vm((micro, rows, feat), bf),
+        vm((micro, rows, feat), bf),
+        dma, dma((2,)), dma((2,)), dma((micro,)),
+    ]
+    scratch += [dma((steps,))] * 8
+    scratch += [dma((4 * micro,))] * 2
+    scratch += [dma((micro * pairs,))] * 4
+    scratch += [dma((2 * micro,))] * 2
+    scratch += [dma((steps,))] * 4
+    work = 2 * micro * rows * width * feat * 5
+    out = pl.pallas_call(
+        lambda *refs: relay_kernel(n_segment, *refs),
+        out_shape=jax.ShapeDtypeStruct((micro, rows, feat), bf),
+        in_specs=[pl.BlockSpec(memory_space=pl.ANY)] * 3,
+        out_specs=pl.BlockSpec(memory_space=pltpu.VMEM),
+        scratch_shapes=scratch,
+        compiler_params=pltpu.CompilerParams(
+            collective_id=0, has_side_effects=True, vmem_limit_bytes=62 * 1024 * 1024),
+        cost_estimate=pl.CostEstimate(flops=work, bytes_accessed=32 << 20, transcendentals=1 << 23),
+        name="relay",
+    )(inbound[0], jnp.transpose(weights[0], (1, 0, 2)), cotangent[0])
+    return out[None]
+
+
 def solution(mesh):
+    sizes = dict(mesh.shape)
+    fused = sizes["dp"] == 2 and sizes["tensor"] == 4
+
+    def run(inbound, weights, cotangent):
+        if fused and inbound.shape[1] == 2 and weights.shape[3] % 512 == 0 and inbound.shape[2] % 256 == 0:
+            return fused_shards(sizes["segment"], inbound, weights, cotangent)
+        return shards(inbound, weights, cotangent)
+
     placed = (
         P("segment", None, "dp", None),
         P("segment", None, None, "tensor"),
         P("segment", None, "dp", "tensor"),
     )
     return jax.shard_map(
-        shards,
+        run,
         mesh=mesh,
         in_specs=placed,
         out_specs=P("segment", None, "dp", "tensor"),

time: 624 us -> 142 us (0.23)
  waiting for transfers between devices: 398 us -> 0 us
  matrix products: 145 us -> 0 us
  Pallas kernels: 0 us -> 140 us
  local copies, waits for them, and re-layouts: 51.2 us -> 2.26 us
  other arithmetic: 15.1 us -> 0 us
  between operations: 13.2 us -> 0.01 us
    psum x2 -> x0, waiting for transfers between devices: 208 us -> none  [the longest x1 122 us: broadcast(): return lax.psum(jnp.where(mine, value, jnp.zeros_like(value)), axis)]
    reduce_scatter x2 -> x0, waiting for transfers between devices: 144 us -> none  [the longest x1 99.1 us: shards(): lax.psum_scatter(joined_grads, 'dp', scatter_dimension=1, tiled=True)]
    pallas_call x0 -> x1, Pallas kernels: none -> 140 us  [fused_shards(): pl.pallas_call(lambda *refs: relay_kernel(n_segment, *refs), out_shape=ja...]
    dot_general x11 -> x0, matrix products: 136 us -> none  [the longest x2 68.8 us: attend(): jnp.einsum('hqk,qhe->khe', score_grad, query_heads, preferred_element_typ...]
    all_gather x1 -> x0, waiting for transfers between devices: 45.5 us -> none  [shards(): all_keyval = lax.all_gather(keyval, 'dp', axis=1, tiled=True)]
    slice x4 -> x0, local copies, waits for them, and re-layouts: 35 us -> none  [the longest x2 34.7 us: shards(): pair_weights = section_layer[:, 1:, :].reshape(model_width, 2 * feat_width)]
    sub x2 -> x0, matrix products: 9.64 us -> none  [attend(): exp_scores = jnp.exp(scores - score_peak)]
    reshape x2 -> x0, local copies, waits for them, and re-layouts: 7.41 us -> none  [shards(): keyval = keyval.reshape(micro_count, row_count, 2, feat_width)]
  transfers between devices with their start and end apart: 5 -> 0, of which waited for: 5 -> 0; matrix products, arithmetic and copies ran while one was open for 7% -> 0% of each run, Pallas kernels for 0% -> 0%
where the time goes in v1:
time: 142 us
  Pallas kernels  140 us (99%)
  local copies, waits for them, and re-layouts  2.26 us (2%)
    pallas_call x1, Pallas kernels, fused_shards(): pl.pallas_call(lambda *refs: relay_kernel(n_segment, *refs), out_shape=ja...  140 us

profile of v1, /device:TPU:0, one launch (start us, length us, event | category | flops | bytes accessed | tf_op | source)
XLA Modules:
  0.0 141.9 jit_solution(10598626434912516753)
XLA Ops:
  0.0 139.6 %relay.1 = bf16[2,256,1024]{2,1,0:T(8,128)(2,1)} custom-call(bf16[2,256,4096]{2,1,0:T(8,128)(2,1)} %bitcast.8, bf16[3,4096,1024]{2,1,0:T(8,128)(2,1)} %bitcast.7, bf16[2,256,1024]{2,1,0:T(8,128)(2,1)} %bitcast.9), custom_call_target="tpu_custom_call" | custom-call | flops 21474836480 | bytes 33554432 | tf_op jit(solution)/shard_map/relay/pallas_call | solution.py:521
  139.6 2.3 %copy.5 = bf16[1,2,256,1024]{3,2,1,0:T(8,128)(2,1)} copy(bf16[1,2,256,1024]{3,2,1,0:T(8,128)(2,1)} %bitcast.6) | data formatting | bytes 2097152

commit v2 on v1

--- a/solution.py
+++ b/solution.py
@@ -112,7 +112,7 @@
     piece = rows // 4
     crow = piece // CHUNKS
     steps = micro * CHUNKS
-    zrow = rows // CHUNKS
+    zrow = feat // CHUNKS
     pairs = half // 128
 
     seg = lax.axis_index("segment")
@@ -229,8 +229,8 @@
             u_copy(i).wait_recv()
             m, row = i // CHUNKS, pl.multiple_of(lax.rem(i, CHUNKS) * zrow, zrow)
             rr = pl.ds(row, zrow)
-            out_ref[m, rr, :] = (z_in[m, rr, :].astype(jnp.float32)
-                                 + cot0[m, rr, :].astype(jnp.float32)).astype(out_ref.dtype)
+            out_ref[m, :, rr] = (z_in[m, rr, :].astype(jnp.float32).T
+                                 + cot0[m, :, rr].astype(jnp.float32)).astype(out_ref.dtype)
             return carry
         lax.fori_loop(0, steps, finish, 0)
 
@@ -263,9 +263,16 @@
             y_copy(j).wait_recv()
             f_copy(j).start()
 
-        x_load.wait()
-
         def q_step(j, carry):
+            forward(j)
+
+            @pl.when(j > 0)
+            def _():
+                relay(j - 1)
+
+            @pl.when(j == 0)
+            def _():
+                x_load.wait()
             q_load(j).wait()
             value = jnp.dot(own_x[...].reshape(micro * rows, width), wq[lax.rem(j, 2)],
                             preferred_element_type=jnp.float32)
@@ -282,11 +289,6 @@
             def _():
                 for m in range(micro):
                     x_copy(0, m).start()
-            forward(j)
-
-            @pl.when(j > 0)
-            def _():
-                relay(j - 1)
             return carry
         lax.fori_loop(0, CHUNKS, q_step, 0)
         for k in range(2):
@@ -373,7 +375,7 @@
             for h, ref in ((d, dkv.at[m, d]), (1 - d, rdkv.at[m])):
                 for k in range(2):
                     part = lax.dot_general(
-                        ref[k], wkv[k, pl.ds(pl.multiple_of(col, half), half), lanes(h, half)],
+                        wkv[k, pl.ds(pl.multiple_of(col, half), half), lanes(h, half)], ref[k],
                         (((1,), (1,)), ((), ())), preferred_element_type=f32)
                     value = part if value is None else value + part
             return value
@@ -387,7 +389,7 @@
             def tile(k, carry):
                 yy, o = k // 2, lax.rem(k, 2)
                 col = (yy * 2 + 1 - c) * feat + o * half
-                core_out[m, yy, :, lanes(o, half)] = term(m, col).astype(jnp.bfloat16)
+                core_out[m, yy, lanes(o, half), :] = term(m, col).astype(jnp.bfloat16)
 
                 @pl.when(o == 1)
                 def _():
@@ -404,20 +406,17 @@
                 def _():
                     k_copy(m, yy).wait_recv()
                 col = (yy * 2 + c) * feat + o * half
-                value = term(m, col) + core_in[m, yy, :, lanes(o, half)].astype(f32)
+                value = term(m, col) + core_in[m, yy, lanes(o, half), :].astype(f32)
 
                 @pl.when(k < 2)
                 def _():
-                    y_out[m, :, lanes(o, half)] = value.astype(jnp.bfloat16)
+                    y_out[m, lanes(o, half), :] = value.astype(jnp.bfloat16)
+                    for q in range(CHUNKS // 2):
+                        v_copy(m * CHUNKS + o * (CHUNKS // 2) + q).start()
 
                 @pl.when(k >= 2)
                 def _():
-                    total[m, :, lanes(o, half)] = value
-
-                @pl.when(k == 1)
-                def _():
-                    for q in range(CHUNKS):
-                        v_copy(m * CHUNKS + q).start()
+                    total[m, lanes(o, half), :] = value
                 return carry
             lax.fori_loop(0, 4, tile, 0)
 
@@ -503,13 +502,13 @@
         vm((micro, rows, half), bf),
         vm((micro, 2, 2, rows, half), bf),
         vm((micro, 2, rows, half), bf),
-        vm((micro, 2, rows, feat), bf),
-        vm((micro, 2, rows, feat), bf),
-        vm((micro, rows, feat), bf),
-        vm((micro, rows, feat), bf),
-        vm((micro, rows, feat), f32),
-        vm((micro, rows, feat), bf),
-        vm((micro, rows, feat), bf),
+        vm((micro, 2, feat, rows), bf),
+        vm((micro, 2, feat, rows), bf),
+        vm((micro, feat, rows), bf),
+        vm((micro, feat, rows), bf),
+        vm((micro, feat, rows), f32),
+        vm((micro, feat, rows), bf),
+        vm((micro, feat, rows), bf),
         dma, dma((2,)), dma((2,)), dma((micro,)),
     ]
     scratch += [dma((steps,))] * 8

time: 142 us -> 140 us (0.986)
  Pallas kernels: 140 us -> 138 us
    pallas_call x1, Pallas kernels: 140 us -> 138 us  [fused_shards(): pl.pallas_call(lambda *refs: relay_kernel(n_segment, *refs), out_shape=ja...]
where the time goes in v2:
time: 140 us
  Pallas kernels  138 us (99%)
  local copies, waits for them, and re-layouts  2.26 us (2%)
    pallas_call x1, Pallas kernels, fused_shards(): pl.pallas_call(lambda *refs: relay_kernel(n_segment, *refs), out_shape=ja...  138 us

profile of v2, /device:TPU:0, one launch (start us, length us, event | category | flops | bytes accessed | tf_op | source)
XLA Modules:
  0.0 139.9 jit_solution(4456054777746968320)
XLA Ops:
  0.0 137.6 %relay.1 = bf16[2,256,1024]{2,1,0:T(8,128)(2,1)} custom-call(bf16[2,256,4096]{2,1,0:T(8,128)(2,1)} %bitcast.8, bf16[3,4096,1024]{2,1,0:T(8,128)(2,1)} %bitcast.7, bf16[2,256,1024]{2,1,0:T(8,128)(2,1)} %bitcast.9), custom_call_target="tpu_custom_call" | custom-call | flops 21474836480 | bytes 33554432 | tf_op jit(solution)/shard_map/relay/pallas_call | solution.py:520
  137.6 2.3 %copy.5 = bf16[1,2,256,1024]{3,2,1,0:T(8,128)(2,1)} copy(bf16[1,2,256,1024]{3,2,1,0:T(8,128)(2,1)} %bitcast.6) | data formatting | bytes 2097152

commit v3 on v2

--- a/solution.py
+++ b/solution.py
@@ -219,6 +219,9 @@
     @pl.when(first)
     def _():
         def send(j, carry):
+            @pl.when(j >= 2)
+            def _():
+                z_copy(x_ref, j - 2).wait_send()
             z_copy(x_ref, j).start()
             return carry
         lax.fori_loop(0, steps, send, 0)
@@ -237,7 +240,7 @@
         def drain(j, carry):
             z_copy(x_ref, j).wait_send()
             return carry
-        lax.fori_loop(0, steps, drain, 0)
+        lax.fori_loop(steps - 2, steps, drain, 0)
 
     @pl.when(jnp.logical_not(first))
     def _():
@@ -366,7 +369,6 @@
                     dkv[m, b, 0, :, lane] = dkb[b]
                     dkv[m, b, 1, :, lane] = dvb[b]
                 d_copy(m, p).start()
-                t_copy(m, p).start()
                 return carry
             lax.fori_loop(lo, hi, pair, 0)
 
@@ -380,45 +382,49 @@
                     value = part if value is None else value + part
             return value
 
-        def grads_out(m):
+        def got_grads(m):
             def got(p, carry):
                 d_copy(m, p).wait_recv()
                 return carry
             lax.fori_loop(0, pairs, got, 0)
 
-            def tile(k, carry):
-                yy, o = k // 2, lax.rem(k, 2)
+        def grads_out(m, yy):
+            def tile(o, carry):
                 col = (yy * 2 + 1 - c) * feat + o * half
                 core_out[m, yy, lanes(o, half), :] = term(m, col).astype(jnp.bfloat16)
-
-                @pl.when(o == 1)
-                def _():
-                    k_copy(m, yy).start()
                 return carry
-            lax.fori_loop(0, 4, tile, 0)
-
-        def grads_in(m):
-            def tile(k, carry):
-                o = lax.rem(k, 2)
-                yy = jnp.where(k < 2, 1 - y, y)
+            lax.fori_loop(0, 2, tile, 0)
+            k_copy(m, yy).start()
+
+        def grads_far(m):
+            k_copy(m, 1 - y).wait_recv()
+
+            def tile(o, carry):
+                col = ((1 - y) * 2 + c) * feat + o * half
+                value = term(m, col) + core_in[m, 1 - y, lanes(o, half), :].astype(f32)
+                y_out[m, lanes(o, half), :] = value.astype(jnp.bfloat16)
 
                 @pl.when(o == 0)
                 def _():
-                    k_copy(m, yy).wait_recv()
-                col = (yy * 2 + c) * feat + o * half
-                value = term(m, col) + core_in[m, yy, lanes(o, half), :].astype(f32)
-
-                @pl.when(k < 2)
-                def _():
-                    y_out[m, lanes(o, half), :] = value.astype(jnp.bfloat16)
                     for q in range(CHUNKS // 2):
-                        v_copy(m * CHUNKS + o * (CHUNKS // 2) + q).start()
-
-                @pl.when(k >= 2)
-                def _():
-                    total[m, lanes(o, half), :] = value
+                        v_copy(m * CHUNKS + q).start()
                 return carry
-            lax.fori_loop(0, 4, tile, 0)
+            lax.fori_loop(0, 2, tile, 0)
+
+        def grads_near(m):
+            k_copy(m, y).wait_recv()
+
+            def tile(o, carry):
+                col = (y * 2 + c) * feat + o * half
+                value = term(m, col) + core_in[m, y, lanes(o, half), :].astype(f32)
+                total[m, lanes(o, half), :] = value
+                return carry
+            lax.fori_loop(0, 2, tile, 0)
+
+        def far_rest(m):
+            for q in range(CHUNKS // 2):
+                v_copy(m * CHUNKS + q).wait_send()
+                v_copy(m * CHUNKS + CHUNKS // 2 + q).start()
 
         def got_parts(m):
             for kind in range(3):
@@ -430,26 +436,48 @@
         attend(0, 0, pairs)
         got_parts(1)
         attend(1, 0, pairs // 2)
-        grads_out(0)
-        attend(1, pairs // 2, pairs)
-        grads_in(0)
-        grads_out(1)
-        grads_in(1)
+        got_grads(0)
+        grads_out(0, 1 - y)
+        grads_out(0, y)
+        grads_far(0)
+        grads_near(0)
+        attend(1, pairs // 2, pairs - 1)
+        far_rest(0)
+        attend(1, pairs - 1, pairs)
 
         def chain(i, carry):
             m, row = i // CHUNKS, pl.multiple_of(lax.rem(i, CHUNKS) * zrow, zrow)
             rr = pl.ds(row, zrow)
             v_copy(i).wait_recv()
-            total[m, rr, :] = total[m, rr, :] + y_in[m, rr, :].astype(f32)
+            value = total[m, rr, :] + y_in[m, rr, :].astype(f32)
+            total[m, rr, :] = value
 
             @pl.when(jnp.logical_not(last))
             def _():
                 u_copy(i).wait_recv()
                 total[m, rr, :] = total[m, rr, :] + z_in[m, rr, :].astype(f32)
             z_out[m, rr, :] = total[m, rr, :].astype(jnp.bfloat16)
+
+            @pl.when(i >= 2)
+            def _():
+                u_copy(i - 2).wait_send()
             u_copy(i).start()
             return carry
-        lax.fori_loop(0, steps, chain, 0)
+
+        got_grads(1)
+        grads_out(1, 1 - y)
+        grads_far(1)
+        lax.fori_loop(0, CHUNKS // 2, chain, 0)
+        grads_out(1, y)
+        lax.fori_loop(CHUNKS // 2, CHUNKS, chain, 0)
+        grads_near(1)
+        far_rest(1)
+
+        def context_out(i, carry):
+            t_copy(i // pairs, lax.rem(i, pairs)).start()
+            return carry
+        lax.fori_loop(0, micro * pairs, context_out, 0)
+        lax.fori_loop(CHUNKS, steps, chain, 0)
 
         def context(i, carry):
             t_copy(i // pairs, lax.rem(i, pairs)).wait_recv()
@@ -466,10 +494,13 @@
             c_copy(i).wait_send()
             y_copy(i).wait_send()
             f_copy(i).wait_send()
-            v_copy(i).wait_send()
+            return carry
+        lax.fori_loop(0, steps, drain, 0)
+        for m in range(micro):
+            for q in range(CHUNKS // 2):
+                v_copy(m * CHUNKS + CHUNKS // 2 + q).wait_send()
+        for i in range(steps - 2, steps):
             u_copy(i).wait_send()
-            return carry
-        lax.fori_loop(0, steps, drain, 0)
 
         def drain_pairs(i, carry):
             d_copy(i // pairs, lax.rem(i, pairs)).wait_send()

time: 140 us -> 132 us (0.943)
  Pallas kernels: 138 us -> 129 us
    pallas_call x1, Pallas kernels: 138 us -> 129 us  [fused_shards(): pl.pallas_call(lambda *refs: relay_kernel(n_segment, *refs), out_shape=ja...]
where the time goes in v3:
time: 132 us
  Pallas kernels  129 us (98%)
  local copies, waits for them, and re-layouts  2.26 us (2%)
    pallas_call x1, Pallas kernels, fused_shards(): pl.pallas_call(lambda *refs: relay_kernel(n_segment, *refs), out_shape=ja...  129 us

profile of v3, /device:TPU:0, one launch (start us, length us, event | category | flops | bytes accessed | tf_op | source)
XLA Modules:
  0.0 131.5 jit_solution(17667947342171368913)
XLA Ops:
  0.0 129.2 %relay.1 = bf16[2,256,1024]{2,1,0:T(8,128)(2,1)} custom-call(bf16[2,256,4096]{2,1,0:T(8,128)(2,1)} %bitcast.8, bf16[3,4096,1024]{2,1,0:T(8,128)(2,1)} %bitcast.7, bf16[2,256,1024]{2,1,0:T(8,128)(2,1)} %bitcast.9), custom_call_target="tpu_custom_call" | custom-call | flops 21474836480 | bytes 33554432 | tf_op jit(solution)/shard_map/relay/pallas_call | solution.py:551
  129.2 2.3 %copy.5 = bf16[1,2,256,1024]{3,2,1,0:T(8,128)(2,1)} copy(bf16[1,2,256,1024]{3,2,1,0:T(8,128)(2,1)} %bitcast.6) | data formatting | bytes 2097152

commit v4 on v3

--- a/solution.py
+++ b/solution.py
@@ -339,30 +339,33 @@
                 lane = lanes(p, 128)
                 key = parts[1, m, 0:2, :, lane].reshape(2 * rows, 128)
                 val = parts[2, m, 0:2, :, lane].reshape(2 * rows, 128)
-                dk = jnp.zeros((2 * rows, 128), f32)
-                dv = jnp.zeros((2 * rows, 128), f32)
+                zero = jnp.zeros((), jnp.bfloat16)
                 masks = [(lane_id < HD), (lane_id >= HD)]
-                zero = jnp.zeros((), jnp.bfloat16)
+                keys = [jnp.where(mask, key, zero) for mask in masks]
+                vals = [jnp.where(mask, val, zero) for mask in masks]
+                both = jnp.concatenate(vals, axis=0)
+                probs, grads, qrys, upss = [], [], [], []
+                nt = (((1,), (1,)), ((), ()))
                 for b in range(2):
                     qry = parts[0, m, b, :, lane]
                     ups = parts[3, m, b, :, lane]
-                    acc = jnp.zeros((128, rows), f32)
-                    for mask in masks:
-                        km = jnp.where(mask, key, zero)
-                        vm = jnp.where(mask, val, zero)
-                        nt = (((1,), (1,)), ((), ()))
+                    for mask, km, vm in zip(masks, keys, vals):
                         sc = lax.dot_general(km, qry, nt, preferred_element_type=f32)
                         dp = lax.dot_general(vm, ups, nt, preferred_element_type=f32)
                         ex = jnp.exp(sc - jnp.max(sc, axis=0, keepdims=True))
                         pr = ex * (1.0 / jnp.sum(ex, axis=0, keepdims=True))
-                        pb = pr.astype(jnp.bfloat16)
                         delta = jnp.sum(pr * dp, axis=0, keepdims=True)
-                        sg = (pr * (dp - delta)).astype(jnp.bfloat16)
-                        acc = acc + lax.dot_general(vm, pb, (((0,), (0,)), ((), ())),
-                                                    preferred_element_type=f32)
-                        dv = dv + jnp.dot(pb, jnp.where(mask, ups, zero), preferred_element_type=f32)
-                        dk = dk + jnp.dot(sg, jnp.where(mask, qry, zero), preferred_element_type=f32)
+                        probs.append(pr.astype(jnp.bfloat16))
+                        grads.append((pr * (dp - delta)).astype(jnp.bfloat16))
+                        qrys.append(jnp.where(mask, qry, zero))
+                        upss.append(jnp.where(mask, ups, zero))
+                    acc = lax.dot_general(both, jnp.concatenate(probs[-2:], axis=0),
+                                          (((0,), (0,)), ((), ())), preferred_element_type=f32)
                     ctx[m, b, :, lane] = acc.T.astype(jnp.bfloat16)
+                dv = jnp.dot(jnp.concatenate(probs, axis=1), jnp.concatenate(upss, axis=0),
+                             preferred_element_type=f32)
+                dk = jnp.dot(jnp.concatenate(grads, axis=1), jnp.concatenate(qrys, axis=0),
+                             preferred_element_type=f32)
                 dkb = dk.astype(jnp.bfloat16).reshape(2, rows, 128)
                 dvb = dv.astype(jnp.bfloat16).reshape(2, rows, 128)
                 for b in range(2):

time: 132 us -> 131 us (level)
  no operation moved by 1% of the time
where the time goes in v4:
time: 131 us
  Pallas kernels  129 us (98%)
  local copies, waits for them, and re-layouts  2.26 us (2%)
    pallas_call x1, Pallas kernels, fused_shards(): pl.pallas_call(lambda *refs: relay_kernel(n_segment, *refs), out_shape=ja...  129 us

profile of v4, /device:TPU:0, one launch (start us, length us, event | category | flops | bytes accessed | tf_op | source)
XLA Modules:
  0.0 130.8 jit_solution(10999796281761140086)
XLA Ops:
  0.0 128.6 %relay.1 = bf16[2,256,1024]{2,1,0:T(8,128)(2,1)} custom-call(bf16[2,256,4096]{2,1,0:T(8,128)(2,1)} %bitcast.8, bf16[3,4096,1024]{2,1,0:T(8,128)(2,1)} %bitcast.7, bf16[2,256,1024]{2,1,0:T(8,128)(2,1)} %bitcast.9), custom_call_target="tpu_custom_call" | custom-call | flops 21474836480 | bytes 33554432 | tf_op jit(solution)/shard_map/relay/pallas_call | solution.py:554
  128.6 2.3 %copy.5 = bf16[1,2,256,1024]{3,2,1,0:T(8,128)(2,1)} copy(bf16[1,2,256,1024]{3,2,1,0:T(8,128)(2,1)} %bitcast.6) | data formatting | bytes 2097152
